TPU v7x, 256 devices: a whole 4x4x8 slice. The times are simulated.
256 devices in a mesh: blk: 64 (over x, z, y_hi), rep: 4 (over y_lo, core).
Axes of the slice: x: 4, y: 4 (y_hi: 2, y_lo: 2; y = y_hi * 2 + y_lo), z: 8, core: 2. Of those that a mesh axis runs over, the one named last changes fastest.
Arguments:
- activated_neurons: bfloat16 [8192, 4304], P('blk', 'rep'), may hold values from -6 to 6
- skip_stream_input: bfloat16 [8192, 1152], P('blk'), may hold values from -6 to 6
- downward_projection_weights: bfloat16 [2, 4304, 1152], P(None, 'rep'), may hold values from -0.09375 to 0.09375
- description_cluster_id: int32 [8192], P('blk'), may hold values from 0 to 2047, as said below
- score_warmth_param: float32 [1], replicated, may hold values from 5 to 20
- score_shift_term: float32 [1], replicated, may hold values from -4 to -1
Outputs:
- hidden_grad: bfloat16 [8192, 4304], P('blk', 'rep')
- weight_grad: float32 [2, 4304, 1152], P(None, 'rep', 'blk')
- loss: float32 [1], replicated
Inputs may be any that keep to these rules, and one draw needn't show every extreme that they name: `description_cluster_id`: among the first 6144 rows every caption id appears exactly 3 times; among the last 2048 rows every caption id appears exactly once.
All inputs are finite; a program needn't handle non-finite values.
Results may differ from a plain program's by a relative error of at most 0.024.
Values may be sent and summed in bfloat16 or wider, within the bound.
A program may use at most 128 MiB of HBM per device.

v0:
```python
import jax
import jax.numpy as jnp
from jax import lax
from jax.sharding import PartitionSpec as P

EPS = 1e-06
OBJECTIVE_SCALE = 16.0


def embed_rows(res_rows, branch):
    pre = res_rows.astype(jnp.float32) + branch
    row_norm = jnp.sqrt(jnp.sum(pre * pre, axis=1, keepdims=True) + EPS)
    unit_rows = pre / row_norm
    return (unit_rows, unit_rows.astype(jnp.bfloat16), row_norm)


def unit_backward(unit_rows, emb_grad, row_norm):
    return (emb_grad - unit_rows * jnp.sum(unit_rows * emb_grad, axis=1, keepdims=True)) / row_norm


def build_folder(
    feature_matrix,
    resident_description_id,
    resident_encoder,
    picture_total,
    sharpness_factor,
    start_position,
):

    def pair_folder(state_pair, visitor, first_row):
        v_emb, v_ids = visitor
        piece_rows = v_emb.shape[0]

        def work(current):
            cosine_match = lax.dot_general(
                feature_matrix, v_emb, (((1,), (1,)), ((), ())), preferred_element_type=jnp.float32
            )
            couple_scores = sharpness_factor * cosine_match + start_position
            v_tower = (jnp.arange(piece_rows, dtype=jnp.int32) >= picture_total).astype(jnp.int32)
            cross_pair = v_tower[None, :] != resident_encoder
            desired_signs = jnp.where(
                resident_description_id[:, None] == v_ids[None, :],
                jnp.float32(1.0),
                jnp.float32(-1.0),
            )
            loss_terms = jnp.where(cross_pair, jax.nn.softplus(-desired_signs * couple_scores), 0.0)
            couple_weight_factor = jnp.where(
                cross_pair,
                -desired_signs
                * jax.nn.sigmoid(-desired_signs * couple_scores)
                * (OBJECTIVE_SCALE * sharpness_factor),
                0.0,
            ).astype(jnp.bfloat16)
            grad_sum = jnp.dot(couple_weight_factor, v_emb, preferred_element_type=jnp.float32)
            loss_part = jnp.where(resident_encoder == 0, jnp.sum(loss_terms), jnp.float32(0.0))
            return (grad_sum, loss_part)

        same_side = jnp.where(
            resident_encoder == 0,
            first_row + piece_rows <= picture_total,
            first_row >= picture_total,
        )
        return lax.cond(same_side, lambda current: current, work, state_pair)

    return pair_folder


def local(
    activated_neurons,
    skip_stream_input,
    downward_projection_weights,
    description_cluster_id,
    score_warmth_param,
    score_shift_term,
):
    row_count = activated_neurons.shape[0]
    width = skip_stream_input.shape[1]
    n_blk = lax.axis_size("blk")
    picture_total = row_count * n_blk * 3 // 4
    blk_pos = lax.axis_index("blk")
    resident_encoder = (blk_pos >= n_blk * 3 // 4).astype(jnp.int32)
    w_mine = lax.dynamic_index_in_dim(
        downward_projection_weights, resident_encoder, 0, keepdims=False
    )
    partial_value = jnp.dot(activated_neurons, w_mine, preferred_element_type=jnp.float32)
    sharpness_factor = score_warmth_param[0]
    start_position = score_shift_term[0]
    branch = lax.psum(partial_value.astype(jnp.bfloat16), "rep").astype(jnp.float32)
    unit_rows, feature_matrix, row_norm = embed_rows(skip_stream_input, branch)
    pair_folder = build_folder(
        feature_matrix,
        description_cluster_id,
        resident_encoder,
        picture_total,
        sharpness_factor,
        start_position,
    )
    initial = (jnp.zeros((row_count, width), jnp.float32), jnp.zeros((), jnp.float32))
    emb_grad, loss_part = pair_folder(
        initial,
        (
            lax.all_gather(feature_matrix, "blk", axis=0, tiled=True),
            lax.all_gather(description_cluster_id, "blk", axis=0, tiled=True),
        ),
        jnp.int32(0),
    )
    loss_all = lax.psum(loss_part, "blk")
    pre_grad = unit_backward(unit_rows, emb_grad, row_norm).astype(jnp.bfloat16)
    hidden_grad = lax.dot_general(
        pre_grad, w_mine, (((1,), (1,)), ((), ())), preferred_element_type=jnp.float32
    ).astype(jnp.bfloat16)
    local_grad = lax.dot_general(
        activated_neurons, pre_grad, (((0,), (0,)), ((), ())), preferred_element_type=jnp.float32
    )
    stacked = jnp.stack(
        [
            jnp.where(resident_encoder == 0, local_grad, 0.0),
            jnp.where(resident_encoder == 1, local_grad, 0.0),
        ],
        axis=0,
    )
    weight_grad = lax.psum_scatter(stacked, "blk", scatter_dimension=2, tiled=True)
    loss_out = jnp.reshape(loss_all / picture_total, (1,))
    return (hidden_grad, weight_grad, loss_out)


def solution(mesh):
    placed = (P("blk", "rep"), P("blk", None), P(None, "rep", None), P("blk"), P(), P())
    return jax.shard_map(
        local,
        mesh=mesh,
        in_specs=placed,
        out_specs=(P("blk", "rep"), P(None, "rep", "blk"), P()),
        check_vma=False,
    )
```

profile of v0, /device:TPU:0, one launch (start us, length us, event | category | flops | bytes accessed | tf_op | source)
XLA Modules:
  0.0 1062.4 jit_solution(2243423324978123176)
XLA Ops:
  7.2 0.0 copy-start
  7.2 0.0 all-reduce.4.cloned.1.call-start
  7.2 6.5 constant_dynamic-slice_fusion.1
  13.7 0.0 copy-start.1
  13.7 2.2 copy-done.1
  15.9 0.0 copy-done
  15.9 0.0 copy-start.3
  15.9 0.0 copy-start.4
  15.9 1.6 fusion.4
  17.5 0.0 all-reduce.4.cloned.1.call-update
  17.6 0.0 all-gather.3.cloned.1.call-start
  17.6 0.0 copy-done.3
  17.6 0.2 copy.18
  17.8 42.7 %all-reduce.4.cloned.1.call-done = bf16[128,1152]{0,1:T(8,128)(2,1)} async-done(((bf16[128,1152]{0,1:T(8,128)(2,1)}), bf16[128,1152]{0,1:T(8,128)(2,1)}) %all-reduce.4.cloned.1.call-update) | async-done | bytes 294928 | tf_op jit(solution)/shard_map/psum | solution.py:88
  60.5 1.1 multiply_reduce_fusion.1
  61.7 1.8 fusion.17
  63.5 0.0 all-gather.3.cloned.1.call-update
  63.5 0.0 all-reduce.6.cloned.1.call-start
  64.8 0.0 copy-done.4
  64.8 181.0 %all-gather = s32[64,1,128]{2,1,0:T(1,128)S(1)} all-gather(s32[1,1,128]{2,1,0:T(1,128)S(1)} %bitcast.30), channel_id=1, replica_groups=mesh['blk'=64,'rep'=4] {'blk'}, dimensions={0}, use_global_device_ids=true | all-gather | bytes 33280 | tf_op jit(solution)/shard_map/all_gather | solution.py:103
  245.8 17.7 %all-gather.3.cloned.1.call-done = bf16[8192,1152]{0,1:T(8,128)(2,1)} async-done(((bf16[128,1152]{0,1:T(8,128)(2,1)}), bf16[8192,1152]{0,1:T(8,128)(2,1)}) %all-gather.3.cloned.1.call-update) | async-done | bytes 18874384 | tf_op jit(solution)/shard_map/all_gather | solution.py:102
  263.5 0.0 copy-start.2
  263.5 0.0 copy-start.5
  263.5 15.4 %fusion.3 = (f32[]{:T(128)}, f32[128,8192]{1,0:T(8,128)}) fusion(pred[8192]{0:T(1024)(128)(4,1)S(1)} %convert_compare_fusion, f32[]{:T(128)} %bitcast.27, bf16[128,1152]{0,1:T(8,128)(2,1)} %fusion.17, bf16[8192,1152]{0,1:T(8,128)(2,1)} %all-gather.3.cloned.1.call-done, f32[]{:T(128)} %bitcast.25, s32[8192]{0:T(1024)S(1)} %bitcast.28, s32[128]{0:T(128)S(1)} %copy-done.4), kind=kOutput, calls=%fused_computation.8 | convolution fusion | flops 2430599168 | bytes 23405068 | tf_op jit(solution)/shard_map/cond/branch_0_fun/dot_general | solution.py:35
  278.9 0.0 copy-done.2
  278.9 0.0 copy-done.5
  278.9 7.4 multiply_reduce_fusion
  286.3 0.9 select_bitcast_fusion.1
  287.3 4.4 pad_maximum_fusion
  291.6 18.9 %copy.22 = f32[2,1076,1152]{1,0,2:T(2,128)} copy(f32[2,1076,1152]{2,1,0:T(8,128)} %pad_maximum_fusion) | data formatting | bytes 19832832 | tf_op jit(solution)/shard_map/stack | solution.py:115
  310.6 0.0 copy-start.6
  310.6 0.0 all-reduce.6.cloned.1.call-update
  310.6 0.6 copy-done.6
  311.2 0.6 dynamic-slice
  313.1 182.6 %psum.15 = f32[]{:T(128)} all-reduce(f32[]{:T(128)S(6)} %select_n.61), channel_id=1, replica_groups=mesh['blk'=64,'rep'=4] {'blk'}, use_global_device_ids=true, to_apply=%region_5.6 | all-reduce | flops 1 | bytes 8 | tf_op jit(solution)/shard_map/psum | solution.py:107
  496.4 4.1 convolution_convert_fusion
  500.4 552.7 %all-reduce.6.cloned.1.call-done = f32[2,1076,1152]{1,0,2:T(2,128)} async-done(((f32[2,1076,1152]{1,0,2:T(2,128)}), f32[2,1076,1152]{1,0,2:T(2,128)}) %all-reduce.6.cloned.1.call-update) | async-done | bytes 9916432
  1053.2 1.6 constant_dynamic-slice_fusion
  (2 shorter events, 0.0 us)
Async XLA Ops:
  7.2 8.7 copy-start
  7.2 53.4 %all-reduce.4.cloned.1.call-start = ((), (), s32[]{:S(2)}) async-start(), calls=%async_computation | async-start | bytes 589824 | tf_op jit(solution)/shard_map/psum | solution.py:88
  13.7 2.2 copy-start.1
  15.9 1.7 copy-start.3
  15.9 48.9 %copy-start.4 = (s32[128]{0:T(128)S(1)}, s32[128]{0:T(128)}, u32[]{:S(2)}) copy-start(s32[128]{0:T(128)} %param.9) | copy-start | bytes 1540
  17.6 246.0 %all-gather.3.cloned.1.call-start = ((), (), s32[]{:S(2)}) async-start(), calls=%async_computation.1 | async-start | bytes 19169280 | tf_op jit(solution)/shard_map/all_gather | solution.py:102
  63.5 989.7 %all-reduce.6.cloned.1.call-start = ((), (), s32[]{:S(2)}) async-start(), calls=%async_computation.2 | async-start | bytes 21233664
  263.5 15.4 %copy-start.2 = (bf16[128,1152]{0,1:T(8,128)(2,1)S(1)}, bf16[128,1152]{0,1:T(8,128)(2,1)}, u32[]{:S(2)}) copy-start(bf16[128,1152]{0,1:T(8,128)(2,1)} %all-reduce.4.cloned.1.call-done) | copy-start | bytes 884740
  263.5 15.4 %copy-start.5 = (bf16[8192,1152]{0,1:T(8,128)(2,1)S(1)}, bf16[8192,1152]{0,1:T(8,128)(2,1)}, u32[]{:S(2)}) copy-start(bf16[8192,1152]{0,1:T(8,128)(2,1)} %all-gather.3.cloned.1.call-done) | copy-start | bytes 56623108
  310.6 0.7 copy-start.6
Sparse Core Ops, SparseCore 0:
  17.7 42.8 all-reduce.3
  64.0 199.5 all-gather.2
  310.7 742.3 all-reduce.5
where the time goes:
time: 1060 us
  waiting for transfers between devices  613 us (58%)
  blocking collectives  364 us (34%)
  local copies, waits for them, and re-layouts  30.6 us (3%)
  matrix products  29.4 us (3%)
  between operations  18.2 us (2%)
    unnamed x4, waiting for transfers between devices  553 us
    psum x1, blocking collectives, local(): loss_all = lax.psum(loss_part, 'blk')  183 us
    all_gather x1, blocking collectives, local(): lax.all_gather(description_cluster_id, 'blk', axis=0, tiled=True)  181 us
    psum x1, waiting for transfers between devices, local(): lax.psum(partial_value.astype(jnp.bfloat16), 'rep').astype(jnp.float32)  42.7 us
  transfers between devices with their start and end apart: 3, of which 3 were waited for; matrix products, arithmetic and copies ran while one was open for 0% of the time, Pallas kernels for 0%

commit v1 on v0

v1 whole, which is shorter than its diff:
```python
import functools

import jax
import jax.numpy as jnp
from jax import lax
from jax.experimental import pallas as pl
from jax.experimental.pallas import tpu as pltpu
from jax.sharding import PartitionSpec as P

EPS = 1e-06
OBJECTIVE_SCALE = 16.0
F32 = jnp.float32
BF16 = jnp.bfloat16
MESH = pl.DeviceIdType.MESH
NT = (((1,), (1,)), ((), ()))
TN = (((0,), (0,)), ((), ()))

NX, NZ, NY, NREP = 4, 8, 2, 4
COL = NY * NREP


def split_hi_lo(v):
    hi = v.astype(BF16)
    return hi, (v - hi.astype(F32)).astype(BF16)


def kernel(
    rows,
    width,
    ffq,
    n_img,
    at_ref,
    skip_ref,
    ids_ref,
    warm_ref,
    shift_ref,
    w_hbm,
    hid_ref,
    wg_ref,
    loss_ref,
    w_ref,
    perm_ref,
    aall,
    part,
    rsbuf,
    emb,
    txt,
    gi,
    gt,
    gir,
    gtr,
    tsum,
    tfin,
    hotb,
    gall,
    eacc,
    gts,
    gtz,
    pacc,
    pieces,
    fin,
    unit_ref,
    norm_ref,
    w_sem,
    rs_s,
    rs_r,
    img_s,
    img_r,
    tx_s,
    txt_s,
    txt_r,
    gi_s,
    gi_r,
    gt_s,
    gt_r,
    tf_s,
    tf_r,
    ga_s,
    ga_r,
    gz_s,
    gz_r,
    pc_s,
    pc_r,
    ar_s,
    al_s,
    a_r,
):
    own = rows // NREP
    d18 = width // (NX * NZ * NY)
    slab = width // NZ
    blk = lax.axis_index("blk")
    rep = lax.axis_index("rep")
    x = blk // (NZ * NY)
    z = (blk // NY) % NZ
    yh = blk % NY
    q = yh * NREP + rep
    is_img = x < NX - 1

    def dev(xx, zz, yy, rr):
        return ((xx * NZ + zz) * NY + yy, rr)

    def col_dev(qq):
        return dev(x, z, qq // NREP, qq % NREP)

    def rcopy(src, dst, ssem, rsem, device):
        return pltpu.make_async_remote_copy(
            src_ref=src, dst_ref=dst, send_sem=ssem, recv_sem=rsem, device_id=device, device_id_type=MESH
        )

    here = (blk, rep)

    def arrived(ref, rsem):
        rcopy(ref, ref, rsem, rsem, here).wait_recv()

    def left_us(ref, ssem):
        rcopy(ref, ref, ssem, ssem, here).wait_send()

    w_copy = pltpu.make_async_copy(w_hbm, w_ref, w_sem)
    w_copy.start()

    barrier = pltpu.get_barrier_semaphore()
    peers = [col_dev((q + k) % COL) for k in range(1, COL)]
    peers += [dev(x, (z + k) % NZ, yh, rep) for k in range(1, NZ)]
    peers += [dev((x + k) % NX, z, yy, rep) for k in range(1, NX) for yy in range(NY)]
    for peer in peers:
        pl.semaphore_signal(barrier, inc=1, device_id=peer, device_id_type=MESH)

    aall[z, pl.ds(ffq // 16 * 16, 16), :] = jnp.zeros((16, rows), BF16)
    aall[z, pl.ds(0, ffq), :] = at_ref[...]

    w_copy.wait()
    a_t = aall[z]
    partial = lax.dot_general(a_t, w_ref[...], TN, preferred_element_type=F32)
    part[...] = partial.astype(BF16).reshape(NREP, own, width)

    pl.semaphore_wait(barrier, len(peers))

    for k in range(1, NREP):
        r = (rep + k) % NREP
        rcopy(part.at[r], rsbuf.at[rep], rs_s.at[k], rs_r.at[rep], (blk, r)).start()

    z_r, z_l = (z + 1) % NZ, (z + NZ - 1) % NZ

    def a_step(s):
        right = (z + NZ - s) % NZ
        left = (z + s) % NZ
        if s > 0:
            arrived(aall.at[right], a_r.at[right])
        rcopy(aall.at[right], aall.at[right], ar_s.at[s], a_r.at[right], dev(x, z_r, yh, rep)).start()
        if s < NZ // 2 - 1:
            if s > 0:
                arrived(aall.at[left], a_r.at[left])
            rcopy(aall.at[left], aall.at[left], al_s.at[s], a_r.at[left], dev(x, z_l, yh, rep)).start()

    a_step(0)

    for zz in range(NZ):
        row = lax.broadcasted_iota(jnp.int32, (slab, width), 0)
        col = lax.broadcasted_iota(jnp.int32, (slab, width), 1)
        per_x = NY * d18
        wrap = jnp.zeros_like(row)
        for j in range(1, NX):
            wrap += (row >= j * per_x).astype(jnp.int32)
        source = row + wrap * (per_x * NZ - per_x) + per_x * zz
        perm_ref[pl.ds(zz * slab, slab), :] = jnp.where(source == col, 1.0, 0.0).astype(BF16)

    ids = ids_ref[...]
    feature = lax.broadcasted_iota(jnp.int32, (128, rows), 0)
    wanted = jnp.where(feature < 64, ids >> 6, (ids & 63) + 64)
    hot = jnp.where(feature == wanted, 1.0, 0.0).astype(F32)
    hotb[...] = hot.T.astype(BF16).reshape(NREP, own, 128)

    for k in range(1, NREP):
        r = (rep + k) % NREP
        arrived(rsbuf.at[r], rs_r.at[r])
    my_rows = pl.ds(pl.multiple_of(rep * own, own), own)
    branch = part[rep].astype(F32)
    for k in range(1, NREP):
        branch += rsbuf[(rep + k) % NREP].astype(F32)
    pre = skip_ref[my_rows, :].astype(F32) + branch
    row_norm = jnp.sqrt(jnp.sum(pre * pre, axis=1, keepdims=True) + EPS)
    unit = pre / row_norm
    unit_ref[...] = unit
    norm_ref[...] = jnp.broadcast_to(row_norm, (own, 128))
    emb[q, :, pl.ds(0, width)] = unit.astype(BF16)
    emb[q, :, pl.ds(width, 128)] = hotb[rep]

    warm = warm_ref[0]
    shift = shift_ref[0]
    loss_rows = (own, 128)

    @pl.when(jnp.logical_not(is_img))
    def _():
        for xx in range(NX - 1):
            rcopy(emb.at[q], txt.at[z], tx_s.at[xx], txt_r.at[z], dev(xx, z, yh, rep)).start()
        a_step(1)

    @pl.when(is_img)
    def _():
        for k in range(1, COL):
            qq = (q + k) % COL
            rcopy(emb.at[q], emb.at[q], img_s.at[k], img_r.at[q], col_dev(qq)).start()
        arrived(txt.at[z], txt_r.at[z])
        for k in range(1, NZ):
            zz = (z + k) % NZ
            rcopy(txt.at[z], txt.at[z], txt_s.at[k], txt_r.at[z], dev(x, zz, yh, rep)).start()
        a_step(1)
        for k in range(1, COL):
            qq = (q + k) % COL
            arrived(emb.at[qq], img_r.at[qq])
        for k in range(1, NZ):
            zz = (z + k) % NZ
            arrived(txt.at[zz], txt_r.at[zz])

        n_i, n_t = COL * own, NZ * own
        e_i = emb[...].reshape(n_i, width + 128)
        e_t = txt[...].reshape(n_t, width + 128)
        cosine = lax.dot_general(e_i[:, :width], e_t[:, :width], NT, preferred_element_type=F32)
        same = lax.dot_general(e_i[:, width:], e_t[:, width:], NT, preferred_element_type=F32)
        target = jnp.where(same > 1.5, 1.0, -1.0).astype(F32)
        margin = -target * (warm * cosine + shift)
        decay = jnp.exp(-jnp.abs(margin))
        softplus = jnp.maximum(margin, 0.0) + jnp.log1p(decay)
        sigmoid = jnp.where(margin >= 0.0, 1.0, decay) / (1.0 + decay)
        coef = (-target * sigmoid * (OBJECTIVE_SCALE * warm)).astype(BF16)
        grad_t = lax.dot_general(coef, e_i[:, :width], TN, preferred_element_type=F32)
        gt[...] = grad_t.astype(BF16).reshape(NZ, own, width)
        for k in range(1, NZ):
            zz = (z + k) % NZ
            rcopy(gt.at[zz], gtr.at[z], gt_s.at[k], gt_r.at[z], dev(x, zz, yh, rep)).start()
        grad_i = lax.dot_general(coef, e_t[:, :width], (((1,), (0,)), ((), ())), preferred_element_type=F32)
        gi[:, :, pl.ds(0, width)] = grad_i.astype(BF16).reshape(COL, own, width)
        loss_tile = jnp.sum(softplus, axis=0, keepdims=True)
        loss_tile = jnp.sum(loss_tile, axis=1, keepdims=True)
        l_hi, l_lo = split_hi_lo(jnp.broadcast_to(loss_tile, loss_rows))
        place = lax.broadcasted_iota(jnp.int32, loss_rows, 0)
        code = jnp.where(place == 0, l_hi.astype(F32), jnp.where(place == 1, l_lo.astype(F32), 0.0)).astype(BF16)
        for qq in range(COL):
            gi[qq, :, pl.ds(width, 128)] = code
        for k in range(1, COL):
            qq = (q + k) % COL
            rcopy(gi.at[qq], gir.at[q], gi_s.at[k], gi_r.at[q], col_dev(qq)).start()
        for k in range(1, NZ):
            zz = (z + k) % NZ
            arrived(gtr.at[zz], gt_r.at[zz])
        total = gt[z].astype(F32)
        for k in range(1, NZ):
            total += gtr[(z + k) % NZ].astype(F32)
        tsum[...] = total.astype(BF16)
        rcopy(tsum, tfin.at[x], tf_s, tf_r.at[x], dev(NX - 1, z, yh, rep)).start()

    a_step(2)

    @pl.when(is_img)
    def _():
        for k in range(1, COL):
            qq = (q + k) % COL
            arrived(gir.at[qq], gi_r.at[qq])
        total = gi[q].astype(F32)
        for k in range(1, COL):
            total += gir[(q + k) % COL].astype(F32)
        eacc[...] = total

    @pl.when(jnp.logical_not(is_img))
    def _():
        total = jnp.zeros((own, width), F32)
        for xx in range(NX - 1):
            arrived(tfin.at[xx], tf_r.at[xx])
            total += tfin[xx].astype(F32)
        eacc[:, pl.ds(0, width)] = total
        eacc[:, pl.ds(width, 128)] = jnp.zeros((own, 128), F32)

    emb_grad = eacc[:, pl.ds(0, width)]
    col_loss = jnp.sum(eacc[:, pl.ds(width, 128)], axis=0, keepdims=True)
    unit = unit_ref[...]
    along = jnp.sum(unit * emb_grad, axis=1, keepdims=True)
    pre_grad = ((emb_grad - unit * along) / norm_ref[:, :1]).astype(BF16)
    gall[rep] = pre_grad
    for k in range(1, NREP):
        r = (rep + k) % NREP
        rcopy(gall.at[rep], gall.at[rep], ga_s.at[k], ga_r.at[rep], (blk, r)).start()
    a_step(3)
    for k in range(1, NREP):
        r = (rep + k) % NREP
        arrived(gall.at[r], ga_r.at[r])

    g_block = gall[...].reshape(rows, width)
    g_t = lax.dot_general(perm_ref[...], g_block, NT, preferred_element_type=F32)
    gts[:, pl.ds(0, slab), :] = g_t.astype(BF16).reshape(NZ, slab, rows)
    l_hi, l_lo = split_hi_lo(col_loss)
    place = lax.broadcasted_iota(jnp.int32, (16, 128), 0)
    code = jnp.where(place == 0, l_hi.astype(F32), jnp.where(place == 1, l_lo.astype(F32), 0.0)).astype(BF16)
    for zz in range(NZ):
        gts[zz, pl.ds(slab, 16), :] = code
    for k in range(1, NZ):
        zz = (z + k) % NZ
        rcopy(gts.at[zz], gtz.at[z], gz_s.at[k], gz_r.at[z], dev(x, zz, yh, rep)).start()
    gtz[z] = gts[z]

    hid = lax.dot_general(w_ref[...], g_block, NT, preferred_element_type=F32)
    hid_ref[...] = hid[:ffq, :].astype(BF16)

    arrived(aall.at[(z + NZ // 2) % NZ], a_r.at[(z + NZ // 2) % NZ])
    arrived(aall.at[(z + NZ // 2 - 1) % NZ], a_r.at[(z + NZ // 2 - 1) % NZ])
    for k in range(1, NZ):
        zz = (z + k) % NZ
        arrived(gtz.at[zz], gz_r.at[zz])

    g_cat = jnp.concatenate([gtz[zz, :slab, :] for zz in range(NZ)], axis=1)
    a_cat = jnp.concatenate([aall[zz] for zz in range(NZ)], axis=1)
    pacc[pl.ds(0, slab), :] = lax.dot_general(g_cat, a_cat, NT, preferred_element_type=F32)
    pacc[pl.ds(slab, 16), :] = jnp.zeros((16, pacc.shape[1]), F32)
    plane = gtz[0, pl.ds(slab, 16), :].astype(F32)
    for zz in range(1, NZ):
        plane += gtz[zz, pl.ds(slab, 16), :].astype(F32)
    l_hi, l_lo = split_hi_lo(jnp.sum(plane, axis=0, keepdims=True))
    n_out = NX * NY
    for k in range(n_out):
        pieces[k] = pacc[pl.ds(k * d18, 32), :].astype(BF16)
        tail = pacc[pl.ds(k * d18 + 16, 16), pl.ds(0, 128)]
        tail = jnp.where(place == d18 - 16, l_hi.astype(F32), tail)
        tail = jnp.where(place == d18 - 15, l_lo.astype(F32), tail)
        pieces[k, pl.ds(16, 16), pl.ds(0, 128)] = tail.astype(BF16)
    mine = x * NY + yh
    for j in range(1, n_out):
        k = (mine + j) % n_out
        rcopy(pieces.at[k], fin.at[mine], pc_s.at[j], pc_r.at[mine], dev(k // NY, z, k % NY, rep)).start()
    fin[mine] = pieces[mine]
    for j in range(1, n_out):
        k = (mine + j) % n_out
        arrived(fin.at[k], pc_r.at[k])
    n_img_out = (NX - 1) * NY
    tower = [fin[0].astype(F32), fin[n_img_out].astype(F32)]
    for k in range(1, n_img_out):
        tower[0] += fin[k].astype(F32)
    for k in range(n_img_out + 1, n_out):
        tower[1] += fin[k].astype(F32)
    for t in range(2):
        for d in range(d18):
            wg_ref[d, pl.ds(t, 1), :] = tower[t][d : d + 1, :ffq]
    loss = jnp.zeros((1, 128), F32)
    for xx in range(NX - 1):
        last = fin[xx * NY, pl.ds(16, 16), pl.ds(0, 128)].astype(F32)
        loss += last[d18 - 16 : d18 - 15, :] + last[d18 - 15 : d18 - 14, :]
    loss_ref[0] = loss[0, 0] / n_img

    for k in range(1, NREP):
        left_us(part.at[0], rs_s.at[k])
        left_us(gall.at[0], ga_s.at[k])
    for s in range(NZ // 2):
        left_us(aall.at[0], ar_s.at[s])
    for s in range(NZ // 2 - 1):
        left_us(aall.at[0], al_s.at[s])
    for k in range(1, NZ):
        left_us(gts.at[0], gz_s.at[k])
    for j in range(1, n_out):
        left_us(pieces.at[0], pc_s.at[j])

    @pl.when(is_img)
    def _():
        for k in range(1, COL):
            left_us(emb.at[0], img_s.at[k])
            left_us(gi.at[0], gi_s.at[k])
        for k in range(1, NZ):
            left_us(txt.at[0], txt_s.at[k])
            left_us(gt.at[0], gt_s.at[k])
        left_us(tsum, tf_s)

    @pl.when(jnp.logical_not(is_img))
    def _():
        for xx in range(NX - 1):
            left_us(emb.at[0], tx_s.at[xx])


def local(
    activated_neurons,
    skip_stream_input,
    downward_projection_weights,
    description_cluster_id,
    score_warmth_param,
    score_shift_term,
):
    rows, ffq = activated_neurons.shape
    width = skip_stream_input.shape[1]
    n_blk = lax.axis_size("blk")
    d18 = width // n_blk
    own = rows // NREP
    slab = width // NZ
    ffp = -(-ffq // 16) * 16
    n_img = rows * n_blk * 3 // 4
    is_text = (lax.axis_index("blk") >= n_blk * 3 // 4).astype(jnp.int32)
    w_mine = lax.dynamic_index_in_dim(downward_projection_weights, is_text, 0, keepdims=False)
    w_mine = jnp.pad(w_mine, ((0, ffp - ffq), (0, 0)))
    vmem = pl.BlockSpec(memory_space=pltpu.VMEM)
    smem = pl.BlockSpec(memory_space=pltpu.SMEM)
    dma = pltpu.SemaphoreType.DMA
    hid_t, wg_t, loss = pl.pallas_call(
        functools.partial(kernel, rows, width, ffq, n_img),
        out_shape=(
            jax.ShapeDtypeStruct((ffq, rows), BF16),
            jax.ShapeDtypeStruct((d18, 2, ffq), F32),
            jax.ShapeDtypeStruct((1,), F32),
        ),
        in_specs=[vmem, vmem, vmem, smem, smem, pl.BlockSpec(memory_space=pl.ANY)],
        out_specs=(vmem, vmem, smem),
        scratch_shapes=[
            pltpu.VMEM((ffp, width), BF16),
            pltpu.VMEM((width, width), BF16),
            pltpu.VMEM((NZ, ffp, rows), BF16),
            pltpu.VMEM((NREP, own, width), BF16),
            pltpu.VMEM((NREP, own, width), BF16),
            pltpu.VMEM((COL, own, width + 128), BF16),
            pltpu.VMEM((NZ, own, width + 128), BF16),
            pltpu.VMEM((COL, own, width + 128), BF16),
            pltpu.VMEM((NZ, own, width), BF16),
            pltpu.VMEM((COL, own, width + 128), BF16),
            pltpu.VMEM((NZ, own, width), BF16),
            pltpu.VMEM((own, width), BF16),
            pltpu.VMEM((NX - 1, own, width), BF16),
            pltpu.VMEM((NREP, own, 128), BF16),
            pltpu.VMEM((NREP, own, width), BF16),
            pltpu.VMEM((own, width + 128), F32),
            pltpu.VMEM((NZ, slab + 16, rows), BF16),
            pltpu.VMEM((NZ, slab + 16, rows), BF16),
            pltpu.VMEM((slab + 16, ffp), F32),
            pltpu.VMEM((NX * NY, 32, ffp), BF16),
            pltpu.VMEM((NX * NY, 32, ffp), BF16),
            pltpu.VMEM((own, width), F32),
            pltpu.VMEM((own, 128), F32),
            dma,
            dma((NREP,)),
            dma((NREP,)),
            dma((COL,)),
            dma((COL,)),
            dma((NX,)),
            dma((NZ,)),
            dma((NZ,)),
            dma((COL,)),
            dma((COL,)),
            dma((NZ,)),
            dma((NZ,)),
            dma,
            dma((NX,)),
            dma((NREP,)),
            dma((NREP,)),
            dma((NZ,)),
            dma((NZ,)),
            dma((NX * NY,)),
            dma((NX * NY,)),
            dma((NZ // 2,)),
            dma((NZ // 2,)),
            dma((NZ,)),
        ],
        compiler_params=pltpu.CompilerParams(
            collective_id=0, has_side_effects=True, vmem_limit_bytes=48 * 1024 * 1024
        ),
        cost_estimate=pl.CostEstimate(flops=2 * 10**9, bytes_accessed=10**7, transcendentals=10**6),
    )(
        activated_neurons.T,
        skip_stream_input,
        description_cluster_id.reshape(1, rows),
        score_warmth_param,
        score_shift_term,
        w_mine,
    )
    return hid_t.T, jnp.transpose(wg_t, (1, 2, 0)), loss


def solution(mesh):
    placed = (P("blk", "rep"), P("blk", None), P(None, "rep", None), P("blk"), P(), P())
    return jax.shard_map(
        local,
        mesh=mesh,
        in_specs=placed,
        out_specs=(P("blk", "rep"), P(None, "rep", "blk"), P()),
        check_vma=False,
    )
```

time: 1060 us -> 102 us (0.10)
  the two profiles are of different devices: /device:TPU:0 before, /device:TPU:64 now
where the time goes in v1:
time: 102 us
  Pallas kernels  90.2 us (88%)
  local copies, waits for them, and re-layouts  8.4 us (8%)
  between operations  3.75 us (4%)
    pallas_call x1, Pallas kernels, local(): pl.pallas_call(functools.partial(kernel, rows, width, ffq, n_img), out_sh...  90.2 us
    dynamic_slice x1, local copies, waits for them, and re-layouts, local(): lax.dynamic_index_in_dim(downward_projection_weights, is_text, 0, keepdim...  6.43 us

profile of v1, /device:TPU:64, one launch (start us, length us, event | category | flops | bytes accessed | tf_op | source)
XLA Modules:
  0.0 102.3 jit_solution(8695628367303200765)
XLA Ops:
  0.6 6.4 %constant_dynamic-slice_fusion = bf16[1,1076,1152]{2,0,1:T(2,128)(2,1)S(1)} fusion(bf16[2,1076,1152]{2,0,1:T(2,128)(2,1)} %param.8, s32[]{:T(128)S(6)} %select_n.4), kind=kLoop, calls=%fused_computation.1 | loop fusion | bytes 4958212 | tf_op jit(solution)/shard_map/jit(dynamic_index_in_dim)/dynamic_slice | solution.py:392
  7.1 0.0 copy-start
  7.1 0.0 copy-start.1
  7.1 0.0 copy-start.2
  7.1 0.4 copy.12
  7.5 0.2 pad.4.w_hbm
  9.0 0.0 copy-done
  9.0 0.0 copy-done.1
  9.0 0.0 copy-done.2
  9.0 90.2 %shard_map.85 = (bf16[1076,128]{1,0:T(8,128)(2,1)S(1)}, f32[18,2,1076]{2,1,0:T(2,128)S(1)}, f32[1]{0:T(128)}) custom-call(bf16[1076,128]{1,0:T(8,128)(2,1)S(1)} %bitcast.9, bf16[128,1152]{1,0:T(8,128)(2,1)S(1)} %copy-done, s32[1,128]{1,0:T(1,128)S(1)} %bitcast.10, f32[1]{0:T(128)S(6)} %copy.16.warm_ref, f32[1]{0:T(128)S(6)} %copy.17.shift_ref, ...), custom_call_target="tpu_custom_call" | custom-call | flops 2000000000 | bytes 10000000 | tf_op jit(solution)/shard_map/pallas_call | solution.py:397
  99.2 0.7 copy.18
  99.9 0.7 copy.19
Async XLA Ops:
  7.1 1.9 %copy-start = (bf16[128,1152]{1,0:T(8,128)(2,1)S(1)}, bf16[128,1152]{1,0:T(8,128)(2,1)}, u32[]{:S(2)}) copy-start(bf16[128,1152]{1,0:T(8,128)(2,1)} %skip_ref.1) | copy-start | bytes 884740
  7.1 1.9 %copy-start.1 = (bf16[128,1076]{0,1:T(8,128)(2,1)S(1)}, bf16[128,1076]{0,1:T(8,128)(2,1)}, u32[]{:S(2)}) copy-start(bf16[128,1076]{0,1:T(8,128)(2,1)} %param.6) | copy-start | bytes 826372
  7.1 1.9 %copy-start.2 = (s32[128]{0:T(128)S(1)}, s32[128]{0:T(128)}, u32[]{:S(2)}) copy-start(s32[128]{0:T(128)} %param.9) | copy-start | bytes 1540

commit v2 on v1

v2 whole, which is shorter than its diff:
```python
import functools

import jax
import jax.numpy as jnp
from jax import lax
from jax.experimental import pallas as pl
from jax.experimental.pallas import tpu as pltpu
from jax.sharding import PartitionSpec as P

EPS = 1e-06
OBJECTIVE_SCALE = 16.0
F32 = jnp.float32
BF16 = jnp.bfloat16
MESH = pl.DeviceIdType.MESH
NT = (((1,), (1,)), ((), ()))
TN = (((0,), (0,)), ((), ()))

NX, NZ, NY, NREP = 4, 8, 2, 4
COL = NY * NREP
NYC = 4


def split_hi_lo(v):
    hi = v.astype(BF16)
    return hi, (v - hi.astype(F32)).astype(BF16)


def kernel(
    rows,
    width,
    ffq,
    n_img,
    at_hbm,
    skip_hbm,
    ids_hbm,
    warm_ref,
    shift_ref,
    w_hbm,
    hid_ref,
    wg_ref,
    loss_ref,
    at_ref,
    skip_ref,
    ids_ref,
    wnat,
    w_ref,
    aint,
    perm_ref,
    aall,
    part,
    rsbuf,
    emb,
    txt,
    lbuf,
    gi,
    gir,
    gix_s,
    gix_r,
    gt,
    gtd,
    gtx,
    gtr,
    tsum,
    tfin,
    hotb,
    gall,
    eacc,
    gts,
    gtz,
    pacc,
    remf,
    pieces,
    fin,
    unit_ref,
    norm_ref,
    w_sem,
    in_sem,
    rs_s,
    rs_r,
    im_s,
    im_r,
    tx_s,
    tt_s,
    tt_r,
    l_s,
    l_r,
    gi_s,
    gi_r,
    gx_s,
    gx_r,
    gd_s,
    gd_r,
    gt_s,
    gt_r,
    tf_s,
    tf_r,
    ga_s,
    ga_r,
    gz_s,
    gz_r,
    gf_s,
    gf_r,
    pc_s,
    pc_r,
    ar_s,
    al_s,
    a_r,
):
    own = rows // NREP
    d18 = width // (NX * NZ * NY)
    slab = width // NZ
    blk = lax.axis_index("blk")
    rep = lax.axis_index("rep")
    x = blk // (NZ * NY)
    z = (blk // NY) % NZ
    yh = blk % NY
    y = yh * 2 + rep // 2
    core = rep % 2
    other = 1 - core
    par = z % 2
    sign = 1 - 2 * par
    z_pair = z + 1 - 2 * par
    is_img = x < NX - 1

    def dev(xx, zz, yy, rr):
        return ((xx * NZ + zz) * NY + yy, rr)

    def z_at(offset):
        return (z + NZ + offset) % NZ

    def at_y(xx, zz, yy, cc):
        return dev(xx, zz, yy // 2, (yy % 2) * 2 + cc)

    def rcopy(src, dst, ssem, rsem, device):
        return pltpu.make_async_remote_copy(
            src_ref=src, dst_ref=dst, send_sem=ssem, recv_sem=rsem, device_id=device, device_id_type=MESH
        )

    here = (blk, rep)

    def arrived(ref, rsem):
        rcopy(ref, ref, rsem, rsem, here).wait_recv()

    sent = {"all": [], "img": [], "txt": []}

    def send(group, src, dst, ssem, rsem, device):
        sem, k = ssem
        rcopy(src, dst, sem if k is None else sem.at[k], rsem, device).start()
        base = src.ref if hasattr(src, "ref") else src
        entry = (base, len(base.shape) - len(src.shape), sem, k)
        if all(e[2] is not sem or e[3] != k for e in sent[group]):
            sent[group].append(entry)

    def all_left(group):
        for ref, block, sem, k in sent[group]:
            ref = ref.at[(0,) * block] if block else ref
            sem = sem if k is None else sem.at[k]
            rcopy(ref, ref, sem, sem, here).wait_send()

    barrier = pltpu.get_barrier_semaphore()
    peers = [at_y(x, z, (y + k) % NYC, core) for k in range(1, NYC)]
    peers += [dev(x, z, yh, (rep // 2) * 2 + other), dev(x, z, yh, (1 - rep // 2) * 2 + other)]
    peers += [dev(x, (z + k) % NZ, yh, rep) for k in range(1, NZ)]
    peers += [dev((x + k) % NX, z, yy, rep) for k in range(1, NX) for yy in range(NY)]
    for peer in peers:
        pl.semaphore_signal(barrier, inc=1, device_id=peer, device_id_type=MESH)

    a_copy = pltpu.make_async_copy(at_hbm, at_ref, in_sem.at[0])
    a_copy.start()
    n_cut = 2
    step = ffq // n_cut
    cuts = [pl.ds(c * step, step) for c in range(n_cut)]
    w_copies = [pltpu.make_async_copy(w_hbm.at[cut], wnat.at[cut], w_sem.at[c]) for c, cut in enumerate(cuts)]
    for copy in w_copies:
        copy.start()
    skip_copy = pltpu.make_async_copy(skip_hbm, skip_ref, in_sem.at[1])
    ids_copy = pltpu.make_async_copy(ids_hbm, ids_ref, in_sem.at[2])
    skip_copy.start()
    ids_copy.start()

    aint[...] = jnp.zeros_like(aint)
    a_copy.wait()
    for t in range(2):

        @pl.when(is_img if t == 0 else jnp.logical_not(is_img))
        def _():
            aint[pl.ds(t, ffq, stride=2), :] = at_ref[...].astype(F32)

    a_int = aint[...].astype(BF16)
    aall[z, pl.ds(ffq // 16 * 16, 16), :] = jnp.zeros((16, rows), BF16)
    aall[z, pl.ds(0, ffq), :] = at_ref[...]
    partial = jnp.zeros((rows, width), F32)
    for c, copy in enumerate(w_copies):
        copy.wait()
        both = pl.ds(2 * c * step, 2 * step)
        w_ref[both, :] = wnat[cuts[c]].reshape(2 * step, width)
        partial += lax.dot_general(a_int[2 * c * step : 2 * (c + 1) * step], w_ref[both, :], TN, preferred_element_type=F32)
    part[...] = partial.astype(BF16).reshape(NREP, own, width)

    pl.semaphore_wait(barrier, len(peers))

    for k in range(1, NREP):
        r = (rep + k) % NREP
        send("all", part.at[r], rsbuf.at[rep], (rs_s, k), rs_r.at[rep], (blk, r))

    z_r, z_l = (z + 1) % NZ, (z + NZ - 1) % NZ

    def a_step(s):
        right = (z + NZ - s) % NZ
        left = (z + s) % NZ
        if s > 0:
            arrived(aall.at[right], a_r.at[right])
        send("all", aall.at[right], aall.at[right], (ar_s, s), a_r.at[right], dev(x, z_r, yh, rep))
        if s < NZ // 2 - 1:
            if s > 0:
                arrived(aall.at[left], a_r.at[left])
            send("all", aall.at[left], aall.at[left], (al_s, s), a_r.at[left], dev(x, z_l, yh, rep))

    def finish():
        all_left("all")

        @pl.when(is_img)
        def _():
            all_left("img")

        @pl.when(jnp.logical_not(is_img))
        def _():
            all_left("txt")

    a_step(0)

    part_rows = (slab + 16) // 2
    row = lax.broadcasted_iota(jnp.int32, (part_rows, width), 0) + core * part_rows
    col = lax.broadcasted_iota(jnp.int32, (part_rows, width), 1)
    per_x = NY * d18
    wrap = jnp.zeros_like(row)
    for k in range(1, NX):
        wrap += (row >= k * per_x).astype(jnp.int32)
    source = row + wrap * (per_x * NZ - per_x)
    for zz in range(NZ):
        perm_ref[pl.ds(zz * part_rows, part_rows), :] = jnp.where(source + per_x * zz == col, 1.0, 0.0).astype(BF16)

    ids_copy.wait()
    skip_copy.wait()
    ids = ids_ref[...]
    feature = lax.broadcasted_iota(jnp.int32, (128, rows), 0)
    wanted = jnp.where(feature < 64, ids >> 6, (ids & 63) + 64)
    hot = jnp.where(feature == wanted, 1.0, 0.0).astype(F32)
    hotb[...] = hot.T.astype(BF16).reshape(NREP, own, 128)

    for k in range(1, NREP):
        r = (rep + k) % NREP
        arrived(rsbuf.at[r], rs_r.at[r])
    my_rows = pl.ds(pl.multiple_of(rep * own, own), own)
    branch = part[rep].astype(F32)
    for k in range(1, NREP):
        branch += rsbuf[(rep + k) % NREP].astype(F32)
    pre = skip_ref[my_rows, :].astype(F32) + branch
    row_norm = jnp.sqrt(jnp.sum(pre * pre, axis=1, keepdims=True) + EPS)
    unit = pre / row_norm
    unit_ref[...] = unit
    mine_i = 2 * y + par
    mine_t = 4 * core
    norm_ref[...] = jnp.broadcast_to(row_norm, (own, 128))
    emb[mine_i, :, pl.ds(0, width)] = unit.astype(BF16)
    emb[mine_i, :, pl.ds(width, 128)] = hotb[rep]

    warm = warm_ref[0]
    shift = shift_ref[0]
    loss_rows = (own, 128)

    @pl.when(jnp.logical_not(is_img))
    def _():
        for xx in range(NX - 1):
            send("txt", emb.at[mine_i], txt.at[mine_t], (tx_s, xx), tt_r.at[mine_t], dev(xx, z, yh, rep))
        a_step(1)

    @pl.when(is_img)
    def _():
        send("img", emb.at[mine_i], emb.at[mine_i], (im_s, 0), im_r.at[mine_i], dev(x, z_pair, yh, rep))
        for k in range(1, NYC):
            send("img", emb.at[mine_i], emb.at[mine_i], (im_s, k), im_r.at[mine_i], at_y(x, z, (y + k) % NYC, core))
        arrived(txt.at[mine_t], tt_r.at[mine_t])
        for k in (3, 2, 1):
            zz = z_at(2 * sign if k == 2 else -k * sign)
            send("img", txt.at[mine_t], txt.at[mine_t + k], (tt_s, k), tt_r.at[mine_t + k], dev(x, zz, yh, rep))
        send("img", txt.at[mine_t], txt.at[mine_t], (tt_s, 0), tt_r.at[mine_t], at_y(x, z, y, other))
        pair_i = 2 * y + 1 - par
        arrived(emb.at[pair_i], im_r.at[pair_i])
        for k in range(1, NYC):
            send("img", emb.at[pair_i], emb.at[pair_i], (im_s, 3 + k), im_r.at[pair_i], at_y(x, z, (y + k) % NYC, core))
        a_step(1)
        for k in range(1, NZ // 2):
            slot = mine_t + k
            arrived(txt.at[slot], tt_r.at[slot])
            send("img", txt.at[slot], txt.at[slot], (tt_s, 3 + k), tt_r.at[slot], at_y(x, z, y, other))
        for k in range(1, NYC):
            for p in range(2):
                slot = 2 * ((y + k) % NYC) + p
                arrived(emb.at[slot], im_r.at[slot])
        for k in range(NZ // 2):
            slot = 4 * other + k
            arrived(txt.at[slot], tt_r.at[slot])

        n_i, n_t = COL * own, NZ * own
        e_i = emb[...].reshape(n_i, width + 128)
        e_t = txt[...].reshape(n_t, width + 128)
        cosine = lax.dot_general(e_i[:, :width], e_t[:, :width], NT, preferred_element_type=F32)
        same = lax.dot_general(e_i[:, width:], e_t[:, width:], NT, preferred_element_type=F32)
        target = jnp.where(same > 1.5, 1.0, -1.0).astype(F32)
        margin = -target * (warm * cosine + shift)
        decay = jnp.exp(-jnp.abs(margin))
        softplus = jnp.maximum(margin, 0.0) + jnp.log1p(decay)
        sigmoid = jnp.where(margin >= 0.0, 1.0, decay) / (1.0 + decay)
        coef = (-target * sigmoid * (OBJECTIVE_SCALE * warm)).astype(BF16)
        loss_tile = jnp.sum(softplus, axis=0, keepdims=True)
        loss_tile = jnp.sum(loss_tile, axis=1, keepdims=True)
        lbuf[0] = jnp.broadcast_to(loss_tile, (8, 128))
        send("img", lbuf.at[0], lbuf.at[1], (l_s, None), l_r, at_y(x, z, y, other))
        grad_t = lax.dot_general(coef, e_i[:, :width], TN, preferred_element_type=F32)
        gt[...] = grad_t.astype(BF16).reshape(2, NZ // 2, own, width)
        send("img", gt.at[other], gtd, (gd_s, None), gd_r, at_y(x, z, y, other))
        grad_i = lax.dot_general(coef, e_t[:, :width], (((1,), (0,)), ((), ())), preferred_element_type=F32)
        gi[:, :, :, pl.ds(0, width)] = grad_i.astype(BF16).reshape(NYC, 2, own, width)
        arrived(lbuf.at[1], l_r)
        l_hi, l_lo = split_hi_lo((lbuf[0] + lbuf[1])[:1, :])
        place = lax.broadcasted_iota(jnp.int32, (own, 128), 0)
        code = jnp.where(place == 0, l_hi.astype(F32), jnp.where(place == 1, l_lo.astype(F32), 0.0)).astype(BF16)
        for yy in range(NYC):
            for p in range(2):
                gi[yy, p, :, pl.ds(width, 128)] = code
        for k in range(1, NYC):
            yy = (y + k) % NYC
            send("img", gi.at[yy], gir.at[y], (gi_s, k), gi_r.at[y], at_y(x, z, yy, core))
        arrived(gtd, gd_r)
        gtx[...] = (gt[core].astype(F32) + gtd[...].astype(F32)).astype(BF16)
        for k in (3, 2, 1):
            send("img", gtx.at[k], gtr.at[k], (gt_s, k), gt_r.at[k], dev(x, z_at(-k * sign), yh, rep))
        a_step(2)
        for k in range(1, NYC):
            yy = (y + k) % NYC
            arrived(gir.at[yy], gi_r.at[yy])
        away = gi[y, 1 - par].astype(F32)
        kept = gi[y, par].astype(F32)
        for k in range(1, NYC):
            away += gir[(y + k) % NYC, 1 - par].astype(F32)
            kept += gir[(y + k) % NYC, par].astype(F32)
        gix_s[...] = away.astype(BF16)
        send("img", gix_s, gix_r, (gx_s, None), gx_r, dev(x, z_pair, yh, rep))
        for k in range(1, NZ // 2):
            arrived(gtr.at[k], gt_r.at[k])
        total = gtx[0].astype(F32)
        for k in range(1, NZ // 2):
            total += gtr[k].astype(F32)
        tsum[...] = total.astype(BF16)
        send("img", tsum, tfin.at[x], (tf_s, None), tf_r.at[x], dev(NX - 1, z, yh, rep))
        arrived(gix_r, gx_r)
        eacc[:, pl.ds(0, width)] = kept[:, :width] + gix_r[:, pl.ds(0, width)].astype(F32)
        eacc[:, pl.ds(width, 128)] = kept[:, width:]

    @pl.when(jnp.logical_not(is_img))
    def _():
        a_step(2)
        total = jnp.zeros((own, width), F32)
        for xx in range(NX - 1):
            arrived(tfin.at[xx], tf_r.at[xx])
            total += tfin[xx].astype(F32)
        eacc[:, pl.ds(0, width)] = total
        eacc[:, pl.ds(width, 128)] = jnp.zeros((own, 128), F32)

    emb_grad = eacc[:, pl.ds(0, width)]
    col_loss = jnp.sum(eacc[:, pl.ds(width, 128)], axis=0, keepdims=True)
    unit = unit_ref[...]
    along = jnp.sum(unit * emb_grad, axis=1, keepdims=True)
    pre_grad = ((emb_grad - unit * along) / norm_ref[:, :1]).astype(BF16)
    gall[rep] = pre_grad
    for k in range(1, NREP):
        r = (rep + k) % NREP
        send("all", gall.at[rep], gall.at[rep], (ga_s, k), ga_r.at[rep], (blk, r))
    a_step(3)
    for k in range(1, NREP):
        r = (rep + k) % NREP
        arrived(gall.at[r], ga_r.at[r])

    g_block = gall[...].reshape(rows, width)
    g_t = lax.dot_general(perm_ref[...], g_block, NT, preferred_element_type=F32)
    gts[...] = g_t.astype(BF16).reshape(NZ, part_rows, rows)
    l_hi, l_lo = split_hi_lo(col_loss)
    place = lax.broadcasted_iota(jnp.int32, (16, 128), 0)
    code = jnp.where(place == 0, l_hi.astype(F32), jnp.where(place == 1, l_lo.astype(F32), 0.0)).astype(BF16)

    @pl.when(core == 1)
    def _():
        for zz in range(NZ):
            gts[zz, pl.ds(part_rows - 16, 16), :] = code

    for i, k in enumerate((4, 3, 5, 2, 6, 1, 7)):
        send("all", gts.at[z_at(k)], gtz.at[z, core], (gz_s, i), gz_r.at[z], dev(x, z_at(k), yh, rep))
    gtz[z, core] = gts[z]
    send("all", gtz.at[z, core], gtz.at[z, core], (gf_s, 0), gf_r.at[z], at_y(x, z, y, other))

    aint[...] = lax.dot_general(w_ref[...], g_block, NT, preferred_element_type=F32)
    for t in range(2):

        @pl.when(is_img if t == 0 else jnp.logical_not(is_img))
        def _():
            hid_ref[...] = aint[pl.ds(t, ffq, stride=2), :].astype(BF16)

    arrived(aall.at[(z + NZ // 2) % NZ], a_r.at[(z + NZ // 2) % NZ])
    arrived(aall.at[(z + NZ // 2 - 1) % NZ], a_r.at[(z + NZ // 2 - 1) % NZ])
    for i, k in enumerate((1, 7, 2, 6, 3, 5, 4)):
        zz = z_at(k)
        arrived(gtz.at[zz, core], gz_r.at[zz])
        send("all", gtz.at[zz, core], gtz.at[zz, core], (gf_s, i + 1), gf_r.at[zz], at_y(x, z, y, other))
    for k in range(NZ):
        arrived(gtz.at[z_at(k), other], gf_r.at[z_at(k)])

    rest = slab - part_rows
    g_cat = jnp.concatenate(
        [jnp.concatenate([gtz[zz, 0], gtz[zz, 1, :rest, :]], axis=0) for zz in range(NZ)], axis=1
    )
    a_cat = jnp.concatenate([aall[zz] for zz in range(NZ)], axis=1)
    lanes = pacc.shape[1]
    pacc[:, pl.ds(lanes - 128, 128)] = jnp.zeros((slab, 128), F32)
    pacc[:, pl.ds(0, a_cat.shape[0])] = lax.dot_general(g_cat, a_cat, NT, preferred_element_type=F32)
    plane = gtz[0, 1, pl.ds(rest, 16), :].astype(F32)
    for zz in range(1, NZ):
        plane += gtz[zz, 1, pl.ds(rest, 16), :].astype(F32)
    l_hi, l_lo = split_hi_lo(jnp.sum(plane, axis=0, keepdims=True))
    extra = jnp.where(place == 1, l_hi.astype(F32), jnp.where(place == 2, l_lo.astype(F32), 0.0))
    n_out = NX * NY
    full = lanes // 128 - 1
    for k in range(n_out):
        remf[k, :, pl.ds(128, 128)] = extra
        for i in range(d18 - 16):
            row = k * d18 + 16 + i
            for c in range(full):
                remf[k, pl.ds(8 * i + c, 1), pl.ds(0, 128)] = pacc[pl.ds(row, 1), pl.ds(c * 128, 128)]
            remf[k, pl.ds(8 * i, 1), pl.ds(128, 128)] = pacc[pl.ds(row, 1), pl.ds(full * 128, 128)]
        pieces[k, :, pl.ds(0, lanes)] = pacc[pl.ds(k * d18, 16), :].astype(BF16)
        pieces[k, :, pl.ds(lanes, 256)] = remf[k].astype(BF16)
    mine = x * NY + yh
    for i, (dx, dy) in enumerate(((2, 1), (1, 1), (3, 1), (2, 0), (0, 1), (1, 0), (3, 0))):
        xx, yy = (x + dx) % NX, (yh + dy) % NY
        send("all", pieces.at[xx * NY + yy], fin.at[mine], (pc_s, i), pc_r.at[mine], dev(xx, z, yy, rep))
    fin[mine] = pieces[mine]
    for j in range(1, n_out):
        k = (mine + j) % n_out
        arrived(fin.at[k], pc_r.at[k])
    n_img_out = (NX - 1) * NY
    tower = [fin[0].astype(F32), fin[n_img_out].astype(F32)]
    for k in range(1, n_img_out):
        tower[0] += fin[k].astype(F32)
    for k in range(n_img_out + 1, n_out):
        tower[1] += fin[k].astype(F32)
    for t in range(2):
        for d in range(16):
            wg_ref[d, pl.ds(t, 1), :] = tower[t][d : d + 1, :ffq]
        for i in range(d18 - 16):
            for c in range(full):
                wg_ref[16 + i, pl.ds(t, 1), pl.ds(c * 128, 128)] = tower[t][8 * i + c : 8 * i + c + 1, lanes : lanes + 128]
            last = ffq - full * 128
            wg_ref[16 + i, pl.ds(t, 1), pl.ds(full * 128, last)] = tower[t][8 * i : 8 * i + 1, lanes + 128 : lanes + 128 + last]
    both = tower[0][1, lanes + 128] + tower[0][2, lanes + 128]
    loss_ref[0] = both / (NY * n_img)

    finish()


def local(
    activated_neurons,
    skip_stream_input,
    downward_projection_weights,
    description_cluster_id,
    score_warmth_param,
    score_shift_term,
):
    rows, ffq = activated_neurons.shape
    width = skip_stream_input.shape[1]
    n_blk = lax.axis_size("blk")
    d18 = width // n_blk
    own = rows // NREP
    slab = width // NZ
    ffp = -(-ffq // 16) * 16
    n_img = rows * n_blk * 3 // 4
    lanes = -(-ffq // 128) * 128
    vmem = pl.BlockSpec(memory_space=pltpu.VMEM)
    hbm = pl.BlockSpec(memory_space=pl.ANY)
    smem = pl.BlockSpec(memory_space=pltpu.SMEM)
    dma = pltpu.SemaphoreType.DMA
    hid_t, wg_t, loss = pl.pallas_call(
        functools.partial(kernel, rows, width, ffq, n_img),
        out_shape=(
            jax.ShapeDtypeStruct((ffq, rows), BF16),
            jax.ShapeDtypeStruct((d18, 2, ffq), F32),
            jax.ShapeDtypeStruct((1,), F32),
        ),
        in_specs=[hbm, hbm, hbm, smem, smem, hbm],
        out_specs=(vmem, vmem, smem),
        scratch_shapes=[
            pltpu.VMEM((ffq, rows), BF16),
            pltpu.VMEM((rows, width), BF16),
            pltpu.VMEM((1, rows), jnp.int32),
            pltpu.VMEM((ffq, 2, width), BF16),
            pltpu.VMEM((2 * ffq, width), BF16),
            pltpu.VMEM((2 * ffq, rows), F32),
            pltpu.VMEM((NZ * (slab + 16) // 2, width), BF16),
            pltpu.VMEM((NZ, ffp, rows), BF16),
            pltpu.VMEM((NREP, own, width), BF16),
            pltpu.VMEM((NREP, own, width), BF16),
            pltpu.VMEM((COL, own, width + 128), BF16),
            pltpu.VMEM((NZ, own, width + 128), BF16),
            pltpu.VMEM((2, 8, 128), F32),
            pltpu.VMEM((NYC, 2, own, width + 128), BF16),
            pltpu.VMEM((NYC, 2, own, width + 128), BF16),
            pltpu.VMEM((own, width + 128), BF16),
            pltpu.VMEM((own, width + 128), BF16),
            pltpu.VMEM((2, NZ // 2, own, width), BF16),
            pltpu.VMEM((NZ // 2, own, width), BF16),
            pltpu.VMEM((NZ // 2, own, width), BF16),
            pltpu.VMEM((NZ // 2, own, width), BF16),
            pltpu.VMEM((own, width), BF16),
            pltpu.VMEM((NX - 1, own, width), BF16),
            pltpu.VMEM((NREP, own, 128), BF16),
            pltpu.VMEM((NREP, own, width), BF16),
            pltpu.VMEM((own, width + 128), F32),
            pltpu.VMEM((NZ, (slab + 16) // 2, rows), BF16),
            pltpu.VMEM((NZ, 2, (slab + 16) // 2, rows), BF16),
            pltpu.VMEM((slab, lanes), F32),
            pltpu.VMEM((NX * NY, 16, 256), F32),
            pltpu.VMEM((NX * NY, 16, lanes + 256), BF16),
            pltpu.VMEM((NX * NY, 16, lanes + 256), BF16),
            pltpu.VMEM((own, width), F32),
            pltpu.VMEM((own, 128), F32),
            dma((4,)),
            dma((3,)),
            dma((NREP,)),
            dma((NREP,)),
            dma((7,)),
            dma((COL,)),
            dma((NX,)),
            dma((7,)),
            dma((NZ,)),
            dma,
            dma,
            dma((NYC,)),
            dma((NYC,)),
            dma,
            dma,
            dma,
            dma,
            dma((NZ // 2,)),
            dma((NZ // 2,)),
            dma,
            dma((NX,)),
            dma((NREP,)),
            dma((NREP,)),
            dma((NZ,)),
            dma((NZ,)),
            dma((NZ,)),
            dma((NZ,)),
            dma((NX * NY,)),
            dma((NX * NY,)),
            dma((NZ // 2,)),
            dma((NZ // 2,)),
            dma((NZ,)),
        ],
        compiler_params=pltpu.CompilerParams(
            collective_id=0, has_side_effects=True, vmem_limit_bytes=53 * 1024 * 1024
        ),
        cost_estimate=pl.CostEstimate(flops=2 * 10**9, bytes_accessed=10**7, transcendentals=10**6),
    )(
        activated_neurons.T,
        skip_stream_input,
        description_cluster_id.reshape(1, rows),
        score_warmth_param,
        score_shift_term,
        jnp.transpose(downward_projection_weights, (1, 0, 2)),
    )
    return hid_t.T, jnp.transpose(wg_t, (1, 2, 0)), loss


def solution(mesh):
    placed = (P("blk", "rep"), P("blk", None), P(None, "rep", None), P("blk"), P(), P())
    return jax.shard_map(
        local,
        mesh=mesh,
        in_specs=placed,
        out_specs=(P("blk", "rep"), P(None, "rep", "blk"), P()),
        check_vma=False,
    )
```

time: 102 us -> 77.7 us (0.76)
  the two profiles are of different devices: /device:TPU:64 before, /device:TPU:1 now
where the time goes in v2:
time: 77.7 us; the launch traced here: 77.5 us
  Pallas kernels  70.8 us (91%)
  between operations  3.7 us (5%)
  local copies, waits for them, and re-layouts  2.98 us (4%)
    pallas_call x1, Pallas kernels, local(): pl.pallas_call(functools.partial(kernel, rows, width, ffq, n_img), out_sh...  70.8 us
    unnamed x6, local copies, waits for them, and re-layouts  2.98 us

profile of v2, /device:TPU:1, one launch (start us, length us, event | category | flops | bytes accessed | tf_op | source)
XLA Modules:
  0.0 77.5 jit_solution(2921951457322868799)
XLA Ops:
  1.9 0.0 copy-start
  1.9 0.9 %copy-done = bf16[128,1076]{0,1:T(8,128)(2,1)S(1)} copy-done((bf16[128,1076]{0,1:T(8,128)(2,1)S(1)}, bf16[128,1076]{0,1:T(8,128)(2,1)}, u32[]{:S(2)}) %copy-start) | copy-done | bytes 275480
  2.9 0.0 copy-start.1
  2.9 0.7 copy-done.1
  3.5 70.8 %shard_map.85 = (bf16[1076,128]{1,0:T(8,128)(2,1)S(1)}, f32[18,2,1076]{2,1,0:T(2,128)S(1)}, f32[1]{0:T(128)}) custom-call(bf16[1076,128]{1,0:T(8,128)(2,1)S(1)} %bitcast.7, bf16[128,1152]{1,0:T(8,128)(2,1)} %skip_hbm.1, s32[1,128]{1,0:T(1,128)S(1)} %bitcast.8, f32[1]{0:T(128)S(6)} %copy.12.warm_ref, f32[1]{0:T(128)S(6)} %copy.13.shift_ref, ...), custom_call_target="tpu_custom_call" | custom-call | flops 2000000000 | bytes 10000000 | tf_op jit(solution)/shard_map/pallas_call | solution.py:491
  74.4 0.7 copy.14
  75.1 0.7 copy.15
Async XLA Ops:
  1.9 1.0 %copy-start = (bf16[128,1076]{0,1:T(8,128)(2,1)S(1)}, bf16[128,1076]{0,1:T(8,128)(2,1)}, u32[]{:S(2)}) copy-start(bf16[128,1076]{0,1:T(8,128)(2,1)} %param.6) | copy-start | bytes 826372
  2.9 0.7 copy-start.1

commit v3 on v2

--- a/solution.py
+++ b/solution.py
@@ -53,11 +53,13 @@
     txt,
     lbuf,
     gi,
+    gid,
+    gaway,
+    garr,
+    gsum,
     gir,
     gix_s,
     gix_r,
-    gt,
-    gtd,
     gtx,
     gtr,
     tsum,
@@ -78,12 +80,15 @@
     rs_s,
     rs_r,
     im_s,
+    ic_s,
     im_r,
     tx_s,
     tt_s,
     tt_r,
     l_s,
     l_r,
+    go_s,
+    go_r,
     gi_s,
     gi_r,
     gx_s,
@@ -105,6 +110,7 @@
     ar_s,
     al_s,
     a_r,
+    a2_r,
 ):
     own = rows // NREP
     d18 = width // (NX * NZ * NY)
@@ -187,8 +193,10 @@
             aint[pl.ds(t, ffq, stride=2), :] = at_ref[...].astype(F32)
 
     a_int = aint[...].astype(BF16)
-    aall[z, pl.ds(ffq // 16 * 16, 16), :] = jnp.zeros((16, rows), BF16)
-    aall[z, pl.ds(0, ffq), :] = at_ref[...]
+    a_half = aall.shape[2]
+    aall[z, 1, pl.ds(a_half - 16, 16), :] = jnp.zeros((16, rows), BF16)
+    aall[z, 0] = at_ref[pl.ds(0, a_half), :]
+    aall[z, 1, pl.ds(0, ffq - a_half), :] = at_ref[pl.ds(a_half, ffq - a_half), :]
     partial = jnp.zeros((rows, width), F32)
     for c, copy in enumerate(w_copies):
         copy.wait()
@@ -206,15 +214,16 @@
     z_r, z_l = (z + 1) % NZ, (z + NZ - 1) % NZ
 
     def a_step(s):
-        right = (z + NZ - s) % NZ
-        left = (z + s) % NZ
+        right, left = z_at(-s), z_at(s)
         if s > 0:
             arrived(aall.at[right], a_r.at[right])
-        send("all", aall.at[right], aall.at[right], (ar_s, s), a_r.at[right], dev(x, z_r, yh, rep))
+            arrived(aall.at[left], a_r.at[left])
         if s < NZ // 2 - 1:
-            if s > 0:
-                arrived(aall.at[left], a_r.at[left])
+            send("all", aall.at[right], aall.at[right], (ar_s, s), a_r.at[right], dev(x, z_r, yh, rep))
             send("all", aall.at[left], aall.at[left], (al_s, s), a_r.at[left], dev(x, z_l, yh, rep))
+        else:
+            send("all", aall.at[right, 0], aall.at[right, 0], (ar_s, s), a_r.at[right], dev(x, z_r, yh, rep))
+            send("all", aall.at[left, 1], aall.at[left, 1], (al_s, s), a2_r, dev(x, z_l, yh, rep))
 
     def finish():
         all_left("all")
@@ -259,11 +268,13 @@
     row_norm = jnp.sqrt(jnp.sum(pre * pre, axis=1, keepdims=True) + EPS)
     unit = pre / row_norm
     unit_ref[...] = unit
-    mine_i = 2 * y + par
-    mine_t = 4 * core
+    def image_at(yy, p, cc):
+        return COL * cc + NYC * p + yy
+
+    mine_i = image_at(y, par, core)
     norm_ref[...] = jnp.broadcast_to(row_norm, (own, 128))
-    emb[mine_i, :, pl.ds(0, width)] = unit.astype(BF16)
-    emb[mine_i, :, pl.ds(width, 128)] = hotb[rep]
+    emb[mine_i, :, :, pl.ds(0, width)] = unit.astype(BF16).reshape(2, own // 2, width)
+    emb[mine_i, :, :, pl.ds(width, 128)] = hotb[rep].reshape(2, own // 2, 128)
 
     warm = warm_ref[0]
     shift = shift_ref[0]
@@ -271,38 +282,44 @@
 
     @pl.when(jnp.logical_not(is_img))
     def _():
-        for xx in range(NX - 1):
-            send("txt", emb.at[mine_i], txt.at[mine_t], (tx_s, xx), tt_r.at[mine_t], dev(xx, z, yh, rep))
+        for h in range(2):
+            for xx in (1, 0, 2):
+                send("txt", emb.at[mine_i, h], txt.at[0, h], (tx_s, 2 * xx + h), tt_r.at[0, h], dev(xx, z, yh, rep))
         a_step(1)
 
     @pl.when(is_img)
     def _():
+        def to_core(slot, k):
+            send("img", emb.at[slot], emb.at[slot], (ic_s, k), im_r.at[slot], at_y(x, z, y, other))
+
         send("img", emb.at[mine_i], emb.at[mine_i], (im_s, 0), im_r.at[mine_i], dev(x, z_pair, yh, rep))
-        for k in range(1, NYC):
+        for k in (2, 1, 3):
             send("img", emb.at[mine_i], emb.at[mine_i], (im_s, k), im_r.at[mine_i], at_y(x, z, (y + k) % NYC, core))
-        arrived(txt.at[mine_t], tt_r.at[mine_t])
-        for k in (3, 2, 1):
-            zz = z_at(2 * sign if k == 2 else -k * sign)
-            send("img", txt.at[mine_t], txt.at[mine_t + k], (tt_s, k), tt_r.at[mine_t + k], dev(x, zz, yh, rep))
-        send("img", txt.at[mine_t], txt.at[mine_t], (tt_s, 0), tt_r.at[mine_t], at_y(x, z, y, other))
-        pair_i = 2 * y + 1 - par
+        to_core(mine_i, 0)
+        pair_i = image_at(y, 1 - par, core)
         arrived(emb.at[pair_i], im_r.at[pair_i])
-        for k in range(1, NYC):
+        for k in (2, 1, 3):
             send("img", emb.at[pair_i], emb.at[pair_i], (im_s, 3 + k), im_r.at[pair_i], at_y(x, z, (y + k) % NYC, core))
+        to_core(pair_i, 1)
+        for h in range(2):
+            arrived(txt.at[0, h], tt_r.at[0, h])
+            for k in (3, 2, 1):
+                zz = z_at(2 * sign if k == 2 else -k * sign)
+                send("img", txt.at[0, h], txt.at[k, h], (tt_s, 4 * h + k), tt_r.at[k, h], dev(x, zz, yh, rep))
         a_step(1)
-        for k in range(1, NZ // 2):
-            slot = mine_t + k
-            arrived(txt.at[slot], tt_r.at[slot])
-            send("img", txt.at[slot], txt.at[slot], (tt_s, 3 + k), tt_r.at[slot], at_y(x, z, y, other))
-        for k in range(1, NYC):
-            for p in range(2):
-                slot = 2 * ((y + k) % NYC) + p
+        for i, p in enumerate((par, 1 - par)):
+            for k in (1, 3, 2):
+                slot = image_at((y + k) % NYC, p, core)
                 arrived(emb.at[slot], im_r.at[slot])
-        for k in range(NZ // 2):
-            slot = 4 * other + k
-            arrived(txt.at[slot], tt_r.at[slot])
-
-        n_i, n_t = COL * own, NZ * own
+                to_core(slot, 2 + 3 * i + k - 1)
+        for k in range(COL):
+            slot = COL * other + k
+            arrived(emb.at[slot], im_r.at[slot])
+        for h in range(2):
+            for k in range(1, NZ // 2):
+                arrived(txt.at[k, h], tt_r.at[k, h])
+
+        n_i, n_t = 2 * COL * own, NZ // 2 * own
         e_i = emb[...].reshape(n_i, width + 128)
         e_t = txt[...].reshape(n_t, width + 128)
         cosine = lax.dot_general(e_i[:, :width], e_t[:, :width], NT, preferred_element_type=F32)
@@ -310,52 +327,60 @@
         target = jnp.where(same > 1.5, 1.0, -1.0).astype(F32)
         margin = -target * (warm * cosine + shift)
         decay = jnp.exp(-jnp.abs(margin))
-        softplus = jnp.maximum(margin, 0.0) + jnp.log1p(decay)
         sigmoid = jnp.where(margin >= 0.0, 1.0, decay) / (1.0 + decay)
         coef = (-target * sigmoid * (OBJECTIVE_SCALE * warm)).astype(BF16)
+        grad_i = lax.dot_general(coef, e_t[:, :width], (((1,), (0,)), ((), ())), preferred_element_type=F32)
+        gi[...] = grad_i.astype(BF16).reshape(2, 2, NYC, own, width)
+        for i, p in enumerate((1 - par, par)):
+            send("img", gi.at[other, p], gid.at[i], (gd_s, i), gd_r.at[i], at_y(x, z, y, other))
+        grad_t = lax.dot_general(coef, e_i[:, :width], TN, preferred_element_type=F32)
+        gtx[...] = grad_t.astype(BF16).reshape(NZ // 2, 2, own // 2, width)
+        for h in range(2):
+            for k in (3, 2, 1):
+                send("img", gtx.at[k, h], gtr.at[k, h], (gt_s, 4 * h + k), gt_r.at[k, h], dev(x, z_at(-k * sign), yh, rep))
+        softplus = jnp.maximum(margin, 0.0) + jnp.log1p(decay)
         loss_tile = jnp.sum(softplus, axis=0, keepdims=True)
         loss_tile = jnp.sum(loss_tile, axis=1, keepdims=True)
         lbuf[0] = jnp.broadcast_to(loss_tile, (8, 128))
         send("img", lbuf.at[0], lbuf.at[1], (l_s, None), l_r, at_y(x, z, y, other))
-        grad_t = lax.dot_general(coef, e_i[:, :width], TN, preferred_element_type=F32)
-        gt[...] = grad_t.astype(BF16).reshape(2, NZ // 2, own, width)
-        send("img", gt.at[other], gtd, (gd_s, None), gd_r, at_y(x, z, y, other))
-        grad_i = lax.dot_general(coef, e_t[:, :width], (((1,), (0,)), ((), ())), preferred_element_type=F32)
-        gi[:, :, :, pl.ds(0, width)] = grad_i.astype(BF16).reshape(NYC, 2, own, width)
+        arrived(gid.at[0], gd_r.at[0])
+        gaway[...] = (gi[core, 1 - par].astype(F32) + gid[0].astype(F32)).astype(BF16)
+        for k in (2, 1, 3):
+            yy = (y + k) % NYC
+            send("img", gaway.at[yy], garr.at[y], (go_s, k), go_r.at[y], at_y(x, z, yy, core))
         arrived(lbuf.at[1], l_r)
         l_hi, l_lo = split_hi_lo((lbuf[0] + lbuf[1])[:1, :])
         place = lax.broadcasted_iota(jnp.int32, (own, 128), 0)
         code = jnp.where(place == 0, l_hi.astype(F32), jnp.where(place == 1, l_lo.astype(F32), 0.0)).astype(BF16)
+        arrived(gid.at[1], gd_r.at[1])
+        gsum[:, :, pl.ds(0, width)] = (gi[core, par].astype(F32) + gid[1].astype(F32)).astype(BF16)
         for yy in range(NYC):
-            for p in range(2):
-                gi[yy, p, :, pl.ds(width, 128)] = code
+            gsum[yy, :, pl.ds(width, 128)] = code
+        for k in (2, 1, 3):
+            yy = (y + k) % NYC
+            send("img", gsum.at[yy], gir.at[y], (gi_s, k), gi_r.at[y], at_y(x, z, yy, core))
+        a_step(2)
+        away = gaway[y].astype(F32)
         for k in range(1, NYC):
             yy = (y + k) % NYC
-            send("img", gi.at[yy], gir.at[y], (gi_s, k), gi_r.at[y], at_y(x, z, yy, core))
-        arrived(gtd, gd_r)
-        gtx[...] = (gt[core].astype(F32) + gtd[...].astype(F32)).astype(BF16)
-        for k in (3, 2, 1):
-            send("img", gtx.at[k], gtr.at[k], (gt_s, k), gt_r.at[k], dev(x, z_at(-k * sign), yh, rep))
-        a_step(2)
+            arrived(garr.at[yy], go_r.at[yy])
+            away += garr[yy].astype(F32)
+        gix_s[...] = away.astype(BF16)
+        send("img", gix_s, gix_r, (gx_s, None), gx_r, dev(x, z_pair, yh, rep))
+        for h in range(2):
+            total = gtx[0, h].astype(F32)
+            for k in range(1, NZ // 2):
+                arrived(gtr.at[k, h], gt_r.at[k, h])
+                total += gtr[k, h].astype(F32)
+            tsum[h] = total.astype(BF16)
+            send("img", tsum.at[h], tfin.at[x, h], (tf_s, h), tf_r.at[x, h], dev(NX - 1, z, yh, rep))
+        kept = gsum[y].astype(F32)
         for k in range(1, NYC):
             yy = (y + k) % NYC
             arrived(gir.at[yy], gi_r.at[yy])
-        away = gi[y, 1 - par].astype(F32)
-        kept = gi[y, par].astype(F32)
-        for k in range(1, NYC):
-            away += gir[(y + k) % NYC, 1 - par].astype(F32)
-            kept += gir[(y + k) % NYC, par].astype(F32)
-        gix_s[...] = away.astype(BF16)
-        send("img", gix_s, gix_r, (gx_s, None), gx_r, dev(x, z_pair, yh, rep))
-        for k in range(1, NZ // 2):
-            arrived(gtr.at[k], gt_r.at[k])
-        total = gtx[0].astype(F32)
-        for k in range(1, NZ // 2):
-            total += gtr[k].astype(F32)
-        tsum[...] = total.astype(BF16)
-        send("img", tsum, tfin.at[x], (tf_s, None), tf_r.at[x], dev(NX - 1, z, yh, rep))
+            kept += gir[yy].astype(F32)
         arrived(gix_r, gx_r)
-        eacc[:, pl.ds(0, width)] = kept[:, :width] + gix_r[:, pl.ds(0, width)].astype(F32)
+        eacc[:, pl.ds(0, width)] = kept[:, :width] + gix_r[...].astype(F32)
         eacc[:, pl.ds(width, 128)] = kept[:, width:]
 
     @pl.when(jnp.logical_not(is_img))
@@ -363,8 +388,9 @@
         a_step(2)
         total = jnp.zeros((own, width), F32)
         for xx in range(NX - 1):
-            arrived(tfin.at[xx], tf_r.at[xx])
-            total += tfin[xx].astype(F32)
+            for h in range(2):
+                arrived(tfin.at[xx, h], tf_r.at[xx, h])
+            total += tfin[xx].reshape(own, width).astype(F32)
         eacc[:, pl.ds(0, width)] = total
         eacc[:, pl.ds(width, 128)] = jnp.zeros((own, 128), F32)
 
@@ -406,8 +432,9 @@
         def _():
             hid_ref[...] = aint[pl.ds(t, ffq, stride=2), :].astype(BF16)
 
-    arrived(aall.at[(z + NZ // 2) % NZ], a_r.at[(z + NZ // 2) % NZ])
-    arrived(aall.at[(z + NZ // 2 - 1) % NZ], a_r.at[(z + NZ // 2 - 1) % NZ])
+    far = z_at(NZ // 2)
+    arrived(aall.at[far, 0], a_r.at[far])
+    arrived(aall.at[far, 1], a2_r)
     for i, k in enumerate((1, 7, 2, 6, 3, 5, 4)):
         zz = z_at(k)
         arrived(gtz.at[zz, core], gz_r.at[zz])
@@ -419,7 +446,7 @@
     g_cat = jnp.concatenate(
         [jnp.concatenate([gtz[zz, 0], gtz[zz, 1, :rest, :]], axis=0) for zz in range(NZ)], axis=1
     )
-    a_cat = jnp.concatenate([aall[zz] for zz in range(NZ)], axis=1)
+    a_cat = jnp.concatenate([aall[zz].reshape(2 * a_half, rows) for zz in range(NZ)], axis=1)
     lanes = pacc.shape[1]
     pacc[:, pl.ds(lanes - 128, 128)] = jnp.zeros((slab, 128), F32)
     pacc[:, pl.ds(0, a_cat.shape[0])] = lax.dot_general(g_cat, a_cat, NT, preferred_element_type=F32)
@@ -481,7 +508,7 @@
     d18 = width // n_blk
     own = rows // NREP
     slab = width // NZ
-    ffp = -(-ffq // 16) * 16
+    ffp = -(-ffq // 32) * 32
     n_img = rows * n_blk * 3 // 4
     lanes = -(-ffq // 128) * 128
     vmem = pl.BlockSpec(memory_space=pltpu.VMEM)
@@ -505,22 +532,24 @@
             pltpu.VMEM((2 * ffq, width), BF16),
             pltpu.VMEM((2 * ffq, rows), F32),
             pltpu.VMEM((NZ * (slab + 16) // 2, width), BF16),
-            pltpu.VMEM((NZ, ffp, rows), BF16),
+            pltpu.VMEM((NZ, 2, ffp // 2, rows), BF16),
             pltpu.VMEM((NREP, own, width), BF16),
             pltpu.VMEM((NREP, own, width), BF16),
-            pltpu.VMEM((COL, own, width + 128), BF16),
-            pltpu.VMEM((NZ, own, width + 128), BF16),
+            pltpu.VMEM((2 * COL, 2, own // 2, width + 128), BF16),
+            pltpu.VMEM((NZ // 2, 2, own // 2, width + 128), BF16),
             pltpu.VMEM((2, 8, 128), F32),
-            pltpu.VMEM((NYC, 2, own, width + 128), BF16),
-            pltpu.VMEM((NYC, 2, own, width + 128), BF16),
-            pltpu.VMEM((own, width + 128), BF16),
-            pltpu.VMEM((own, width + 128), BF16),
-            pltpu.VMEM((2, NZ // 2, own, width), BF16),
-            pltpu.VMEM((NZ // 2, own, width), BF16),
-            pltpu.VMEM((NZ // 2, own, width), BF16),
-            pltpu.VMEM((NZ // 2, own, width), BF16),
+            pltpu.VMEM((2, 2, NYC, own, width), BF16),
+            pltpu.VMEM((2, NYC, own, width), BF16),
+            pltpu.VMEM((NYC, own, width), BF16),
+            pltpu.VMEM((NYC, own, width), BF16),
+            pltpu.VMEM((NYC, own, width + 128), BF16),
+            pltpu.VMEM((NYC, own, width + 128), BF16),
             pltpu.VMEM((own, width), BF16),
-            pltpu.VMEM((NX - 1, own, width), BF16),
+            pltpu.VMEM((own, width), BF16),
+            pltpu.VMEM((NZ // 2, 2, own // 2, width), BF16),
+            pltpu.VMEM((NZ // 2, 2, own // 2, width), BF16),
+            pltpu.VMEM((2, own // 2, width), BF16),
+            pltpu.VMEM((NX - 1, 2, own // 2, width), BF16),
             pltpu.VMEM((NREP, own, 128), BF16),
             pltpu.VMEM((NREP, own, width), BF16),
             pltpu.VMEM((own, width + 128), F32),
@@ -538,21 +567,24 @@
             dma((NREP,)),
             dma((7,)),
             dma((COL,)),
-            dma((NX,)),
-            dma((7,)),
+            dma((2 * COL,)),
+            dma((2 * (NX - 1),)),
             dma((NZ,)),
+            dma((NZ // 2, 2)),
             dma,
             dma,
             dma((NYC,)),
             dma((NYC,)),
+            dma((NYC,)),
+            dma((NYC,)),
             dma,
             dma,
-            dma,
-            dma,
-            dma((NZ // 2,)),
-            dma((NZ // 2,)),
-            dma,
-            dma((NX,)),
+            dma((2,)),
+            dma((2,)),
+            dma((NZ,)),
+            dma((NZ // 2, 2)),
+            dma((2,)),
+            dma((NX - 1, 2)),
             dma((NREP,)),
             dma((NREP,)),
             dma((NZ,)),
@@ -564,9 +596,10 @@
             dma((NZ // 2,)),
             dma((NZ // 2,)),
             dma((NZ,)),
+            dma,
         ],
         compiler_params=pltpu.CompilerParams(
-            collective_id=0, has_side_effects=True, vmem_limit_bytes=53 * 1024 * 1024
+            collective_id=0, has_side_effects=True, vmem_limit_bytes=53 * 1024 * 1024 + 512 * 1024
         ),
         cost_estimate=pl.CostEstimate(flops=2 * 10**9, bytes_accessed=10**7, transcendentals=10**6),
     )(

time: 77.7 us -> 74.8 us (0.963)
  Pallas kernels: 70.8 us -> 69 us
  local copies, waits for them, and re-layouts: 2.98 us -> 2.02 us
    pallas_call x1, Pallas kernels: 70.8 us -> 69 us  [local(): pl.pallas_call(functools.partial(kernel, rows, width, ffq, n_img), out_sh...]
    unnamed x6 -> x4, local copies, waits for them, and re-layouts: 2.98 us -> 2.02 us
where the time goes in v3:
time: 74.8 us; the launch traced here: 74.7 us
  Pallas kernels  69 us (92%)
  between operations  3.7 us (5%)
  local copies, waits for them, and re-layouts  2.02 us (3%)
    pallas_call x1, Pallas kernels, local(): pl.pallas_call(functools.partial(kernel, rows, width, ffq, n_img), out_sh...  69 us
    unnamed x4, local copies, waits for them, and re-layouts  2.02 us

profile of v3, /device:TPU:1, one launch (start us, length us, event | category | flops | bytes accessed | tf_op | source)
XLA Modules:
  0.0 74.7 jit_solution(4474991987075456598)
XLA Ops:
  1.9 0.0 copy-start
  1.9 0.6 copy-done
  2.6 69.0 %shard_map.85 = (bf16[1076,128]{1,0:T(8,128)(2,1)S(1)}, f32[18,2,1076]{2,1,0:T(2,128)S(1)}, f32[1]{0:T(128)}) custom-call(bf16[1076,128]{1,0:T(8,128)(2,1)} %bitcast.9, bf16[128,1152]{1,0:T(8,128)(2,1)} %skip_hbm.1, s32[1,128]{1,0:T(1,128)S(1)} %bitcast.7, f32[1]{0:T(128)S(6)} %copy.12.warm_ref, f32[1]{0:T(128)S(6)} %copy.13.shift_ref, ...), custom_call_target="tpu_custom_call" | custom-call | flops 2000000000 | bytes 10000000 | tf_op jit(solution)/shard_map/pallas_call | solution.py:518
  71.6 0.7 copy.14
  72.3 0.7 copy.15
Async XLA Ops:
  1.9 0.7 copy-start

commit v4 on v3

--- a/solution.py
+++ b/solution.py
@@ -425,13 +425,6 @@
     gtz[z, core] = gts[z]
     send("all", gtz.at[z, core], gtz.at[z, core], (gf_s, 0), gf_r.at[z], at_y(x, z, y, other))
 
-    aint[...] = lax.dot_general(w_ref[...], g_block, NT, preferred_element_type=F32)
-    for t in range(2):
-
-        @pl.when(is_img if t == 0 else jnp.logical_not(is_img))
-        def _():
-            hid_ref[...] = aint[pl.ds(t, ffq, stride=2), :].astype(BF16)
-
     far = z_at(NZ // 2)
     arrived(aall.at[far, 0], a_r.at[far])
     arrived(aall.at[far, 1], a2_r)
@@ -471,6 +464,13 @@
         xx, yy = (x + dx) % NX, (yh + dy) % NY
         send("all", pieces.at[xx * NY + yy], fin.at[mine], (pc_s, i), pc_r.at[mine], dev(xx, z, yy, rep))
     fin[mine] = pieces[mine]
+    aint[...] = lax.dot_general(w_ref[...], gall[...].reshape(rows, width), NT, preferred_element_type=F32)
+    for t in range(2):
+
+        @pl.when(is_img if t == 0 else jnp.logical_not(is_img))
+        def _():
+            hid_ref[...] = aint[pl.ds(t, ffq, stride=2), :].astype(BF16)
+
     for j in range(1, n_out):
         k = (mine + j) % n_out
         arrived(fin.at[k], pc_r.at[k])

time: 74.8 us -> 74.6 us (level)
  no operation moved by 1% of the time
where the time goes in v4:
time: 74.6 us; the launch traced here: 74.5 us
  Pallas kernels  68.7 us (92%)
  between operations  3.7 us (5%)
  local copies, waits for them, and re-layouts  2.02 us (3%)
    pallas_call x1, Pallas kernels, local(): pl.pallas_call(functools.partial(kernel, rows, width, ffq, n_img), out_sh...  68.7 us
    unnamed x4, local copies, waits for them, and re-layouts  2.02 us

profile of v4, /device:TPU:1, one launch (start us, length us, event | category | flops | bytes accessed | tf_op | source)
XLA Modules:
  0.0 74.5 jit_solution(13765770260891453942)
XLA Ops:
  1.9 0.0 copy-start
  1.9 0.6 copy-done
  2.6 68.7 %shard_map.85 = (bf16[1076,128]{1,0:T(8,128)(2,1)S(1)}, f32[18,2,1076]{2,1,0:T(2,128)S(1)}, f32[1]{0:T(128)}) custom-call(bf16[1076,128]{1,0:T(8,128)(2,1)} %bitcast.9, bf16[128,1152]{1,0:T(8,128)(2,1)} %skip_hbm.1, s32[1,128]{1,0:T(1,128)S(1)} %bitcast.7, f32[1]{0:T(128)S(6)} %copy.12.warm_ref, f32[1]{0:T(128)S(6)} %copy.13.shift_ref, ...), custom_call_target="tpu_custom_call" | custom-call | flops 2000000000 | bytes 10000000 | tf_op jit(solution)/shard_map/pallas_call | solution.py:518
  71.3 0.7 copy.14
  72.0 0.7 copy.15
Async XLA Ops:
  1.9 0.7 copy-start
